TPU v7x, 256 devices: a whole 4x4x8 slice. The times are simulated.
256 devices in a mesh: row: 32 (over y, x, core), col: 8 (over z).
Axes of the slice: x: 4, y: 4, z: 8, core: 2. Of those that a mesh axis runs over, the one named last changes fastest.
Arguments:
- features: bfloat16 [524288, 256], P(('row', 'col')), may hold values from -6 to 6
- w_self: bfloat16 [256, 256], replicated, may hold values from -0.375 to 0.375
- w_neigh: bfloat16 [256, 256], replicated, may hold values from -1.5 to 1.5
- bias: float32 [256], replicated, may hold values from -3 to 3
- hub_ids: int32 [6], replicated, may hold values from 0 to 31
- hub_adj: bfloat16 [256, 6, 2048, 256], P(('row', 'col')), may hold values from 0 to 2, as said below
- send_tile: int32 [256, 8, 2], P(('row', 'col')), may hold values from 0 to 15
- recv_count: int32 [256, 8], P(('row', 'col')), may hold values from 0 to 2, as said below
- recv_dst: int32 [256, 8, 2], P(('row', 'col')), may hold values from 0 to 15
- recv_adj: bfloat16 [256, 8, 2, 128, 128], P(('row', 'col')), may hold values from 0 to 2, as said below
- cotangent: bfloat16 [524288, 256], P(('row', 'col')), may hold values from -6 to 6
Outputs:
- output: bfloat16 [524288, 256], P(('row', 'col'))
- feature_grad: bfloat16 [524288, 256], P(('row', 'col'))
Inputs may be any that keep to these rules, and one draw needn't show every extreme that they name: `recv_count`: every device uses all 2 slots from at least one device of its row group. `hub_adj`: nonnegative edge weights. `recv_adj`: nonnegative edge weights.
All inputs are finite; a program needn't handle non-finite values.
Results may differ from a plain program's by a relative error of at most 0.0055.
Values may be sent and summed in bfloat16 or wider, within the bound.
A program may use at most 64 MiB of HBM per device.

v0:
```python
import jax
import jax.numpy as jnp
from jax import lax
from jax.sharding import PartitionSpec as P


def shards(
    features,
    w_self,
    w_neigh,
    bias,
    hub_ids,
    hub_adj,
    send_tile,
    recv_count,
    recv_dst,
    recv_adj,
    cotangent,
):
    f32 = jnp.float32
    bf16 = jnp.bfloat16
    nodes, width = features.shape
    sections = hub_ids.shape[0]
    hub_rows = hub_adj.shape[3]
    peers, slots, tile = (recv_adj.shape[1], recv_adj.shape[2], recv_adj.shape[3])
    total = peers * slots
    count_tiles = nodes // tile
    adjacency = hub_adj[0]
    rows_n = lax.axis_size("row")
    part = hub_rows // rows_n
    pieces = lax.all_to_all(
        features[:hub_rows].reshape(rows_n, part, width),
        "row",
        split_axis=0,
        concat_axis=0,
        tiled=True,
    )
    picked = jnp.stack(
        [lax.dynamic_index_in_dim(pieces, hub_ids[s], 0, keepdims=False) for s in range(sections)]
    )
    gathered = lax.all_gather(picked, "row", axis=0, tiled=False)
    blocks = jnp.transpose(gathered, (1, 0, 2, 3)).reshape(sections, hub_rows, width)
    hub_sum = jnp.zeros((nodes, width), f32)
    for section in range(sections):
        hub_sum = hub_sum + jnp.dot(adjacency[section], blocks[section], preferred_element_type=f32)
    offered = send_tile[0].reshape(total)
    outgoing = jnp.stack(
        [lax.dynamic_slice_in_dim(features, offered[i] * tile, tile, 0) for i in range(total)]
    ).reshape(peers, slots, tile, width)
    incoming = lax.all_to_all(outgoing, "col", split_axis=0, concat_axis=0, tiled=True)
    live = (
        (jnp.arange(slots, dtype=jnp.int32)[None, :] < recv_count[0][:, None])
        .astype(f32)
        .reshape(total)
    )
    landing = recv_dst[0].reshape(total)
    select = (landing[:, None] == jnp.arange(count_tiles, dtype=jnp.int32)[None, :]).astype(
        f32
    ) * live[:, None]
    weights = recv_adj[0].reshape(total, tile, tile)
    contrib = jnp.einsum(
        "sij,sjd->sid", weights, incoming.reshape(total, tile, width), preferred_element_type=f32
    )
    tile_sum = jnp.einsum("sn,sid->nid", select, contrib, precision=lax.Precision.HIGHEST).reshape(
        nodes, width
    )
    row_weight = jnp.sum(weights.astype(f32), axis=2)
    tile_deg = jnp.einsum("sn,si->ni", select, row_weight, precision=lax.Precision.HIGHEST).reshape(
        nodes
    )
    degree = 1.0 + jnp.sum(adjacency.astype(f32), axis=(0, 2)) + tile_deg
    agg = ((tile_sum + hub_sum) / degree[:, None]).astype(bf16)
    pre = (
        jnp.dot(features, w_self, preferred_element_type=f32)
        + jnp.dot(agg, w_neigh, preferred_element_type=f32)
        + bias
    )
    sig = jax.nn.sigmoid(pre)
    output = (pre * sig).astype(bf16)
    grad = (cotangent.astype(f32) * sig * (1.0 + pre * (1.0 - sig))).astype(bf16)
    contract = (((1,), (1,)), ((), ()))
    self_grad = lax.dot_general(grad, w_self, contract, preferred_element_type=f32)
    agg_grad = (
        lax.dot_general(grad, w_neigh, contract, preferred_element_type=f32) / degree[:, None]
    ).astype(bf16)
    partials = jnp.stack(
        [
            lax.dot_general(
                adjacency[section], agg_grad, (((0,), (0,)), ((), ())), preferred_element_type=f32
            ).astype(bf16)
            for section in range(sections)
        ]
    ).reshape(sections, rows_n, part, width)
    landed = lax.all_to_all(partials, "row", split_axis=1, concat_axis=1, tiled=True)
    summed = jnp.sum(landed.astype(f32), axis=1)
    owners = (hub_ids[None, :] == jnp.arange(rows_n, dtype=jnp.int32)[:, None]).astype(f32)
    to_owner = jnp.sum(owners[:, :, None, None] * summed[None], axis=1).astype(bf16)
    hub_back = (
        lax.all_to_all(to_owner, "row", split_axis=0, concat_axis=0, tiled=True)
        .astype(f32)
        .reshape(hub_rows, width)
    )
    dest_rows = jnp.stack(
        [lax.dynamic_slice_in_dim(agg_grad, landing[i] * tile, tile, 0) for i in range(total)]
    )
    slot_grad = (
        jnp.einsum("sij,sid->sjd", weights, dest_rows, preferred_element_type=f32)
        * live[:, None, None]
    ).astype(bf16)
    returned = lax.all_to_all(
        slot_grad.reshape(peers, slots, tile, width), "col", split_axis=0, concat_axis=0, tiled=True
    )
    owned = (offered[:, None] == jnp.arange(count_tiles, dtype=jnp.int32)[None, :]).astype(f32)
    tile_back = jnp.einsum(
        "sn,sid->nid",
        owned,
        returned.reshape(total, tile, width).astype(f32),
        precision=lax.Precision.HIGHEST,
    ).reshape(nodes, width)
    hub_padded = jnp.concatenate([hub_back, jnp.zeros((nodes - hub_rows, width), f32)], axis=0)
    feature_grad = (self_grad + tile_back + hub_padded).astype(bf16)
    return (output, feature_grad)


def solution(mesh):
    placed = (
        P(("row", "col"), None),
        P(),
        P(),
        P(),
        P(),
        P(("row", "col"), None, None, None),
        P(("row", "col"), None, None),
        P(("row", "col"), None),
        P(("row", "col"), None, None),
        P(("row", "col"), None, None, None, None),
        P(("row", "col"), None),
    )
    return jax.shard_map(
        shards,
        mesh=mesh,
        in_specs=placed,
        out_specs=(P(("row", "col"), None), P(("row", "col"), None)),
        check_vma=False,
    )
```

profile of v0, /device:TPU:1, one launch (start us, length us, event | category | flops | bytes accessed | tf_op | source)
XLA Modules:
  0.0 204.4 jit_solution(7526366855033646529)
XLA Ops:
  0.7 1.7 slice_bitcast_fusion.13
  2.3 8.6 %all-to-all-start.1 = ((bf16[32,8,256]{2,1,0:T(8,128)(2,1)}), bf16[32,8,256]{2,1,0:T(8,128)(2,1)S(1)}, u32[]{:S(2)}, u32[]{:S(2)}) async-start(bf16[32,8,256]{2,1,0:T(8,128)(2,1)} %slice_bitcast_fusion.13), calls=%async_computation.1 | async-start | bytes 262144 | tf_op jit(solution)/shard_map/all_to_all | solution.py:31
  22.6 1.6 fusion.66
  50.9 1.3 copy.133
  52.7 3.7 %convert_reduce_fusion = f32[2048]{0:T(1024)S(1)} fusion(bf16[1,6,2048,256]{3,2,1,0:T(8,128)(2,1)} %param.16), kind=kLoop, calls=%fused_computation | loop fusion | flops 6289408 | bytes 6299648 | tf_op jit(solution)/shard_map/reduce_sum | solution.py:71
  56.4 1.8 fusion.70
  62.2 8.3 %all-to-all-start = ((bf16[8,2,128,256]{2,3,1,0:T(8,128)(2,1)}), bf16[8,2,128,256]{2,3,1,0:T(8,128)(2,1)}, u32[]{:S(2)}, u32[]{:S(2)}) async-start(bf16[8,2,128,256]{2,3,1,0:T(8,128)(2,1)} %copy.133), calls=%async_computation | async-start | bytes 2097152 | tf_op jit(solution)/shard_map/all_to_all | solution.py:50
  70.6 25.5 %all-gather = bf16[192,8,256]{2,1,0:T(8,128)(2,1)S(1)} all-gather(bf16[6,8,256]{2,1,0:T(8,128)(2,1)S(1)} %constant_dynamic-update-slice_fusion.16), channel_id=2, replica_groups=mesh['row'=32,'col'=8] {'row'}, dimensions={0}, use_global_device_ids=true | all-gather | bytes 811008 | tf_op jit(solution)/shard_map/all_gather | solution.py:41
  96.1 1.9 fusion.33
  98.0 1.7 convolution_add_fusion.6
  100.8 1.8 convolution_add_fusion.3
  102.6 3.0 %convolution_bitcast_fusion = f32[16,128,256]{1,2,0:T(8,128)} fusion(bf16[16,128,256]{1,2,0:T(8,128)(2,1)} %bitcast.35, bf16[16,128,128]{2,1,0:T(8,128)(2,1)S(1)} %bitcast.269), kind=kOutput, calls=%fused_computation.21 | convolution fusion | flops 134217728 | bytes 3670016 | tf_op jit(solution)/shard_map/sij,sjd->sid/dot_general | solution.py:61
  105.6 2.2 %copy.134 = f32[16,128,256]{2,0,1:T(8,128)S(1)} copy(f32[16,128,256]{1,2,0:T(8,128)} %convolution_bitcast_fusion) | data formatting | bytes 4194304 | tf_op jit(solution)/shard_map/sij,sjd->sid/dot_general | solution.py:61
  107.9 2.5 %fusion.51 = f32[16,128,256]{2,0,1:T(8,128)S(1)} fusion(f32[16,128,256]{2,0,1:T(8,128)S(1)} %copy.134, f32[16]{0:T(128)} %copy-done.10, s32[16]{0:T(128)S(1)} %eq.45), kind=kOutput, calls=%fused_computation.126 | convolution fusion | flops 100663808 | bytes 4194432 | tf_op jit(solution)/shard_map/sn,sid->nid/dot_general | solution.py:64
  110.4 1.2 copy.135
  111.6 1.9 copy.136
  113.5 6.0 %multiply_convert_fusion.1 = (bf16[2048,256]{1,0:T(8,128)(2,1)S(1)}, bf16[2048,256]{1,0:T(8,128)(2,1)}) fusion(bf16[2048,256]{1,0:T(8,128)(2,1)} %param.21, f32[256]{0:T(256)S(1)} %copy-done.13, f32[2048,256]{1,0:T(8,128)} %fusion.70, bf16[256,256]{1,0:T(8,128)(2,1)S(1)} %copy-done, f32[2048,256]{0,1:T(8,128)} %copy.136, ...), kind=kOutput, calls=%fused_computation.18 | convolution fusion | flops 546308096 | bytes 10757120 | tf_op jit(solution)/shard_map/dot_general | solution.py:75
  120.4 2.8 %fusion.9 = bf16[6,32,8,256]{3,2,0,1:T(8,128)(2,1)} fusion(bf16[2048,256]{0,1:T(8,128)(2,1)S(1)} %fusion.5, bf16[1,6,2048,256]{3,2,1,0:T(8,128)(2,1)} %param.16), kind=kOutput, calls=%fused_computation.31 | convolution fusion | flops 268500992 | bytes 2228224 | tf_op jit(solution)/shard_map/dot_general | solution.py:88
  123.2 2.4 %fusion.11 = bf16[6,32,8,256]{3,2,0,1:T(8,128)(2,1)} fusion(bf16[6,32,8,256]{3,2,0,1:T(8,128)(2,1)} %fusion.9, bf16[2048,256]{0,1:T(8,128)(2,1)S(1)} %fusion.5, bf16[1,6,2048,256]{3,2,1,0:T(8,128)(2,1)} %param.16), kind=kOutput, calls=%fused_computation.33 | convolution fusion | flops 268500992 | bytes 2228224 | tf_op jit(solution)/shard_map/dot_general | solution.py:88
  125.6 2.4 %fusion.13 = bf16[6,32,8,256]{3,2,0,1:T(8,128)(2,1)} fusion(bf16[6,32,8,256]{3,2,0,1:T(8,128)(2,1)} %fusion.11, bf16[2048,256]{0,1:T(8,128)(2,1)S(1)} %fusion.5, bf16[1,6,2048,256]{3,2,1,0:T(8,128)(2,1)} %param.16), kind=kOutput, calls=%fused_computation.35 | convolution fusion | flops 268500992 | bytes 2228224 | tf_op jit(solution)/shard_map/dot_general | solution.py:88
  128.1 2.4 %fusion.15 = bf16[6,32,8,256]{3,2,0,1:T(8,128)(2,1)} fusion(bf16[6,32,8,256]{3,2,0,1:T(8,128)(2,1)} %fusion.13, bf16[2048,256]{0,1:T(8,128)(2,1)S(1)} %fusion.5, bf16[1,6,2048,256]{3,2,1,0:T(8,128)(2,1)} %param.16), kind=kOutput, calls=%fused_computation.37 | convolution fusion | flops 268500992 | bytes 2228224 | tf_op jit(solution)/shard_map/dot_general | solution.py:88
  130.5 2.4 %fusion.17 = bf16[6,32,8,256]{3,2,0,1:T(8,128)(2,1)} fusion(bf16[6,32,8,256]{3,2,0,1:T(8,128)(2,1)} %fusion.15, bf16[2048,256]{0,1:T(8,128)(2,1)S(1)} %fusion.5, bf16[1,6,2048,256]{3,2,1,0:T(8,128)(2,1)} %param.16), kind=kOutput, calls=%fused_computation.39 | convolution fusion | flops 268500992 | bytes 2228224 | tf_op jit(solution)/shard_map/dot_general | solution.py:88
  132.9 2.4 %fusion.19 = bf16[6,32,8,256]{3,2,0,1:T(8,128)(2,1)} fusion(bf16[6,32,8,256]{3,2,0,1:T(8,128)(2,1)} %fusion.17, bf16[2048,256]{0,1:T(8,128)(2,1)S(1)} %fusion.5, bf16[1,6,2048,256]{3,2,1,0:T(8,128)(2,1)} %param.16), kind=kOutput, calls=%fused_computation.41 | convolution fusion | flops 268500992 | bytes 2228224 | tf_op jit(solution)/shard_map/dot_general | solution.py:88
  135.3 5.2 %all-to-all-start.3 = ((bf16[6,32,8,256]{3,2,0,1:T(8,128)(2,1)}), bf16[6,32,8,256]{3,2,0,1:T(8,128)(2,1)S(1)}, u32[]{:S(2)}, u32[]{:S(2)}) async-start(bf16[6,32,8,256]{3,2,0,1:T(8,128)(2,1)} %fusion.19), calls=%async_computation.3 | async-start | bytes 1572864 | tf_op jit(solution)/shard_map/all_to_all | solution.py:94
  144.5 1.4 multiply_convert_fusion
  145.9 8.9 %all-to-all-done.3 = bf16[6,32,8,256]{3,2,0,1:T(8,128)(2,1)S(1)} async-done(((bf16[6,32,8,256]{3,2,0,1:T(8,128)(2,1)}), bf16[6,32,8,256]{3,2,0,1:T(8,128)(2,1)S(1)}, u32[]{:S(2)}, u32[]{:S(2)}) %all-to-all-start.3) | async-done | bytes 786464 | tf_op jit(solution)/shard_map/all_to_all | solution.py:94
  154.8 6.9 %all-to-all-start.2 = ((bf16[8,2,128,256]{2,3,1,0:T(8,128)(2,1)}), bf16[8,2,128,256]{2,3,1,0:T(8,128)(2,1)S(1)}, u32[]{:S(2)}, u32[]{:S(2)}) async-start(bf16[8,2,128,256]{2,3,1,0:T(8,128)(2,1)} %bitcast.98), calls=%async_computation.2 | async-start | bytes 2097152 | tf_op jit(solution)/shard_map/all_to_all | solution.py:110
  162.8 28.2 %all-to-all-done.2 = bf16[8,2,128,256]{2,3,1,0:T(8,128)(2,1)S(1)} async-done(((bf16[8,2,128,256]{2,3,1,0:T(8,128)(2,1)}), bf16[8,2,128,256]{2,3,1,0:T(8,128)(2,1)S(1)}, u32[]{:S(2)}, u32[]{:S(2)}) %all-to-all-start.2) | async-done | bytes 1048608 | tf_op jit(solution)/shard_map/all_to_all | solution.py:110
  190.9 4.3 %all-to-all-start.4 = ((bf16[32,8,256]{2,1,0:T(8,128)(2,1)}), bf16[32,8,256]{2,1,0:T(8,128)(2,1)S(1)}, u32[]{:S(2)}, u32[]{:S(2)}) async-start(bf16[32,8,256]{2,1,0:T(8,128)(2,1)} %multiply_reduce_fusion), calls=%async_computation.4 | async-start | bytes 262144 | tf_op jit(solution)/shard_map/all_to_all | solution.py:99
  196.6 1.2 copy.171
  197.9 5.0 %all-to-all-done.4 = bf16[32,8,256]{2,1,0:T(8,128)(2,1)S(1)} async-done(((bf16[32,8,256]{2,1,0:T(8,128)(2,1)}), bf16[32,8,256]{2,1,0:T(8,128)(2,1)S(1)}, u32[]{:S(2)}, u32[]{:S(2)}) %all-to-all-start.4) | async-done | bytes 131104 | tf_op jit(solution)/shard_map/all_to_all | solution.py:99
  202.9 1.4 fusion.4
  (91 shorter events, 19.7 us)
Async XLA Ops:
  0.6 112.9 %copy-start = (bf16[256,256]{1,0:T(8,128)(2,1)S(1)}, bf16[256,256]{1,0:T(8,128)(2,1)}, u32[]{:S(2)}) copy-start(bf16[256,256]{1,0:T(8,128)(2,1)} %param.13) | copy-start | bytes 393220
  0.6 50.1 %copy-start.1 = (bf16[2048,256]{1,0:T(8,128)(2,1)S(1)}, bf16[2048,256]{1,0:T(8,128)(2,1)}, u32[]{:S(2)}) copy-start(bf16[2048,256]{1,0:T(8,128)(2,1)} %param.11) | copy-start | bytes 3145732
  2.3 59.8 %all-to-all-start.1 = ((bf16[32,8,256]{2,1,0:T(8,128)(2,1)}), bf16[32,8,256]{2,1,0:T(8,128)(2,1)S(1)}, u32[]{:S(2)}, u32[]{:S(2)}) async-start(bf16[32,8,256]{2,1,0:T(8,128)(2,1)} %slice_bitcast_fusion.13), calls=%async_computation.1 | async-start | bytes 262144 | tf_op jit(solution)/shard_map/all_to_all | solution.py:31
  43.1 9.2 %copy-start.12 = (s32[1,8]{1,0:T(1,128)S(1)}, s32[1,8]{1,0:T(1,128)}, u32[]{:S(2)}) copy-start(s32[1,8]{1,0:T(1,128)} %param.18) | copy-start | bytes 100
  43.1 9.3 %copy-start.2 = (bf16[1,8,2,128,128]{4,3,2,1,0:T(8,128)(2,1)S(1)}, bf16[1,8,2,128,128]{4,3,2,1,0:T(8,128)(2,1)}, u32[]{:S(2)}) copy-start(bf16[1,8,2,128,128]{4,3,2,1,0:T(8,128)(2,1)} %param.20) | copy-start | bytes 1572868
  52.4 9.6 %copy-start.10 = (f32[16]{0:T(128)}, f32[16]{0:T(128)S(1)}, u32[]{:S(2)}) copy-start(f32[16]{0:T(128)S(1)} %reshape.208) | copy-start | bytes 196
  52.6 3.7 %copy-start.7 = (bf16[256,256]{1,0:T(8,128)(2,1)S(1)}, bf16[256,256]{1,0:T(8,128)(2,1)}, u32[]{:S(2)}) copy-start(bf16[256,256]{1,0:T(8,128)(2,1)} %param.12) | copy-start | bytes 393220
  62.2 37.6 %slice-start = ((s8[6291456]{0:T(1024)(128)(4,1)}), s8[2097152]{0:T(1024)(128)(4,1)S(1)}, s32[]{:S(2)}) async-start(s8[6291456]{0:T(1024)(128)(4,1)} %bitcast.265), calls=%async_computation.5 | async-start | bytes 4194304
  62.2 40.4 %all-to-all-start = ((bf16[8,2,128,256]{2,3,1,0:T(8,128)(2,1)}), bf16[8,2,128,256]{2,3,1,0:T(8,128)(2,1)}, u32[]{:S(2)}, u32[]{:S(2)}) async-start(bf16[8,2,128,256]{2,3,1,0:T(8,128)(2,1)} %copy.133), calls=%async_computation | async-start | bytes 2097152 | tf_op jit(solution)/shard_map/all_to_all | solution.py:50
  96.1 3.6 %slice-start.1 = ((s8[6291456]{0:T(1024)(128)(4,1)}), s8[4194304]{0:T(1024)(128)(4,1)S(1)}, s32[]{:S(2)}) async-start(s8[6291456]{0:T(1024)(128)(4,1)} %bitcast.265), calls=%async_computation.6 | async-start | bytes 8388608
  111.6 1.9 copy-start.13
  119.5 1.0 copy-start.3
  120.4 12.4 %copy-start.5 = (bf16[2048,256]{0,1:T(8,128)(2,1)}, bf16[2048,256]{0,1:T(8,128)(2,1)S(1)}, u32[]{:S(2)}) copy-start(bf16[2048,256]{0,1:T(8,128)(2,1)S(1)} %fusion.5) | copy-start | bytes 3145732
  135.3 8.7 %copy-start.6 = (bf16[2048,256]{0,1:T(8,128)(2,1)S(1)}, bf16[2048,256]{0,1:T(8,128)(2,1)}, u32[]{:S(2)}) copy-start(bf16[2048,256]{0,1:T(8,128)(2,1)} %copy-done.5) | copy-start | bytes 3145732
  135.3 9.2 %copy-start.11 = (f32[16]{0:T(128)S(1)}, f32[16]{0:T(128)}, u32[]{:S(2)}) copy-start(f32[16]{0:T(128)} %copy-done.10) | copy-start | bytes 196
  135.3 19.5 %all-to-all-start.3 = ((bf16[6,32,8,256]{3,2,0,1:T(8,128)(2,1)}), bf16[6,32,8,256]{3,2,0,1:T(8,128)(2,1)S(1)}, u32[]{:S(2)}, u32[]{:S(2)}) async-start(bf16[6,32,8,256]{3,2,0,1:T(8,128)(2,1)} %fusion.19), calls=%async_computation.3 | async-start | bytes 1572864 | tf_op jit(solution)/shard_map/all_to_all | solution.py:94
  144.5 17.2 %copy-start.9 = (s32[6]{0:T(128)S(1)}, s32[6]{0:T(128)}, u32[]{:S(2)}) copy-start(s32[6]{0:T(128)} %param.15) | copy-start | bytes 76
  154.8 36.2 %all-to-all-start.2 = ((bf16[8,2,128,256]{2,3,1,0:T(8,128)(2,1)}), bf16[8,2,128,256]{2,3,1,0:T(8,128)(2,1)S(1)}, u32[]{:S(2)}, u32[]{:S(2)}) async-start(bf16[8,2,128,256]{2,3,1,0:T(8,128)(2,1)} %bitcast.98), calls=%async_computation.2 | async-start | bytes 2097152 | tf_op jit(solution)/shard_map/all_to_all | solution.py:110
  190.9 12.0 %all-to-all-start.4 = ((bf16[32,8,256]{2,1,0:T(8,128)(2,1)}), bf16[32,8,256]{2,1,0:T(8,128)(2,1)S(1)}, u32[]{:S(2)}, u32[]{:S(2)}) async-start(bf16[32,8,256]{2,1,0:T(8,128)(2,1)} %multiply_reduce_fusion), calls=%async_computation.4 | async-start | bytes 262144 | tf_op jit(solution)/shard_map/all_to_all | solution.py:99
  196.6 6.3 %copy-start.4 = (bf16[2048,256]{1,0:T(8,128)(2,1)S(1)}, bf16[2048,256]{1,0:T(8,128)(2,1)}, u32[]{:S(2)}) copy-start(bf16[2048,256]{1,0:T(8,128)(2,1)} %copy-done.3) | copy-start | bytes 3145732
  196.6 6.3 %copy-start.8 = (bf16[256,256]{1,0:T(8,128)(2,1)S(1)}, bf16[256,256]{1,0:T(8,128)(2,1)}, u32[]{:S(2)}) copy-start(bf16[256,256]{1,0:T(8,128)(2,1)} %param.12) | copy-start | bytes 393220
where the time goes:
time: 206 us; the launch traced here: 204 us
  waiting for transfers between devices  42.1 us (20%)
  matrix products  38.4 us (19%)
  starting transfers between devices  33.4 us (16%)
  between operations  32.4 us (16%)
  local copies, waits for them, and re-layouts  27.4 us (13%)
  blocking collectives  25.5 us (12%)
  other arithmetic  5.07 us (2%)
    all_to_all x1, waiting for transfers between devices, shards(): lax.all_to_all(slot_grad.reshape(peers, slots, tile, width), 'col', split...  28.2 us
    all_gather x1, blocking collectives, shards(): gathered = lax.all_gather(picked, 'row', axis=0, tiled=False)  25.5 us
    dot_general x6, matrix products, shards(): lax.dot_general(adjacency[section], agg_grad, (((0,), (0,)), ((), ())), p...  14.8 us
    unnamed x69, local copies, waits for them, and re-layouts  13.7 us
    all_to_all x1, waiting for transfers between devices, shards(): lax.all_to_all(partials, 'row', split_axis=1, concat_axis=1, tiled=True)  8.89 us
    all_to_all x1, starting transfers between devices, shards(): lax.all_to_all(features[:hub_rows].reshape(rows_n, part, width), 'row', s...  8.59 us
    all_to_all x1, starting transfers between devices, shards(): lax.all_to_all(outgoing, 'col', split_axis=0, concat_axis=0, tiled=True)  8.33 us
    all_to_all x1, starting transfers between devices, shards(): lax.all_to_all(slot_grad.reshape(peers, slots, tile, width), 'col', split...  6.92 us
  transfers between devices with their start and end apart: 5, of which 3 were waited for; matrix products, arithmetic and copies ran while one was open for 17% of the time, Pallas kernels for 0%

commit v1 on v0

--- a/solution.py
+++ b/solution.py
@@ -91,7 +91,9 @@
             for section in range(sections)
         ]
     ).reshape(sections, rows_n, part, width)
-    landed = lax.all_to_all(partials, "row", split_axis=1, concat_axis=1, tiled=True)
+    parts = jnp.split(partials, lax.axis_size("row"), axis=1)
+    received = lax.all_to_all(jnp.stack(parts), "row", 0, 0)
+    landed = jnp.concatenate(received, axis=1)
     summed = jnp.sum(landed.astype(f32), axis=1)
     owners = (hub_ids[None, :] == jnp.arange(rows_n, dtype=jnp.int32)[:, None]).astype(f32)
     to_owner = jnp.sum(owners[:, :, None, None] * summed[None], axis=1).astype(bf16)

time: 206 us -> 221 us (1.073)
  local copies, waits for them, and re-layouts: 27.4 us -> 43.6 us
  matrix products: 38.4 us -> 34.4 us
  waiting for transfers between devices: 42.1 us -> 45.4 us
    unnamed x69 -> x100, local copies, waits for them, and re-layouts: 13.7 us -> 29.3 us
    dot_general x6, matrix products: 14.8 us -> 10.9 us  [shards(): lax.dot_general(adjacency[section], agg_grad, (((0,), (0,)), ((), ())), p...]
    all_to_all x1, waiting for transfers between devices: 8.89 us -> 12.2 us  [shards(): received = lax.all_to_all(jnp.stack(parts), 'row', 0, 0)]
  transfers between devices with their start and end apart: 5 -> 5, of which waited for: 3 -> 3; matrix products, arithmetic and copies ran while one was open for 17% -> 14% of each run, Pallas kernels for 0% -> 0%
where the time goes in v1:
time: 221 us; the launch traced here: 220 us
  waiting for transfers between devices  45.4 us (21%)
  local copies, waits for them, and re-layouts  43.6 us (20%)
  matrix products  34.4 us (16%)
  starting transfers between devices  33.3 us (15%)
  between operations  32.5 us (15%)
  blocking collectives  25.5 us (12%)
  other arithmetic  5.07 us (2%)
    unnamed x100, local copies, waits for them, and re-layouts  29.3 us
    all_to_all x1, waiting for transfers between devices, shards(): lax.all_to_all(slot_grad.reshape(peers, slots, tile, width), 'col', split...  28.2 us
    all_gather x1, blocking collectives, shards(): gathered = lax.all_gather(picked, 'row', axis=0, tiled=False)  25.5 us
    all_to_all x1, waiting for transfers between devices, shards(): received = lax.all_to_all(jnp.stack(parts), 'row', 0, 0)  12.2 us
    dot_general x6, matrix products, shards(): lax.dot_general(adjacency[section], agg_grad, (((0,), (0,)), ((), ())), p...  10.9 us
    all_to_all x1, starting transfers between devices, shards(): lax.all_to_all(features[:hub_rows].reshape(rows_n, part, width), 'row', s...  8.59 us
    all_to_all x1, starting transfers between devices, shards(): lax.all_to_all(outgoing, 'col', split_axis=0, concat_axis=0, tiled=True)  8.33 us
    all_to_all x1, starting transfers between devices, shards(): lax.all_to_all(slot_grad.reshape(peers, slots, tile, width), 'col', split...  6.92 us
  transfers between devices with their start and end apart: 5, of which 3 were waited for; matrix products, arithmetic and copies ran while one was open for 14% of the time, Pallas kernels for 0%

profile of v1, /device:TPU:1, one launch (start us, length us, event | category | flops | bytes accessed | tf_op | source)
XLA Modules:
  0.0 219.8 jit_solution(4971217499120939832)
XLA Ops:
  0.7 1.7 slice_bitcast_fusion.13
  2.3 8.6 %all-to-all-start.1 = ((bf16[32,8,256]{2,1,0:T(8,128)(2,1)}), bf16[32,8,256]{2,1,0:T(8,128)(2,1)S(1)}, u32[]{:S(2)}, u32[]{:S(2)}) async-start(bf16[32,8,256]{2,1,0:T(8,128)(2,1)} %slice_bitcast_fusion.13), calls=%async_computation.1 | async-start | bytes 262144 | tf_op jit(solution)/shard_map/all_to_all | solution.py:31
  22.6 1.6 fusion.66
  50.9 1.3 copy.245
  52.7 3.7 %convert_reduce_fusion = f32[2048]{0:T(1024)S(1)} fusion(bf16[1,6,2048,256]{3,2,1,0:T(8,128)(2,1)} %param.16), kind=kLoop, calls=%fused_computation | loop fusion | flops 6289408 | bytes 6299648 | tf_op jit(solution)/shard_map/reduce_sum | solution.py:71
  56.4 1.8 fusion.70
  62.2 8.3 %all-to-all-start = ((bf16[8,2,128,256]{2,3,1,0:T(8,128)(2,1)}), bf16[8,2,128,256]{2,3,1,0:T(8,128)(2,1)}, u32[]{:S(2)}, u32[]{:S(2)}) async-start(bf16[8,2,128,256]{2,3,1,0:T(8,128)(2,1)} %copy.245), calls=%async_computation | async-start | bytes 2097152 | tf_op jit(solution)/shard_map/all_to_all | solution.py:50
  70.6 25.5 %all-gather = bf16[192,8,256]{2,1,0:T(8,128)(2,1)S(1)} all-gather(bf16[6,8,256]{2,1,0:T(8,128)(2,1)S(1)} %constant_dynamic-update-slice_fusion.16), channel_id=2, replica_groups=mesh['row'=32,'col'=8] {'row'}, dimensions={0}, use_global_device_ids=true | all-gather | bytes 811008 | tf_op jit(solution)/shard_map/all_gather | solution.py:41
  96.1 1.9 fusion.33
  98.0 1.7 convolution_add_fusion.6
  100.8 1.8 convolution_add_fusion.3
  102.6 3.0 %convolution_bitcast_fusion = f32[16,128,256]{1,2,0:T(8,128)} fusion(bf16[16,128,256]{1,2,0:T(8,128)(2,1)} %bitcast.35, bf16[16,128,128]{2,1,0:T(8,128)(2,1)S(1)} %bitcast.447), kind=kOutput, calls=%fused_computation.21 | convolution fusion | flops 134217728 | bytes 3670016 | tf_op jit(solution)/shard_map/sij,sjd->sid/dot_general | solution.py:61
  105.6 2.2 %copy.246 = f32[16,128,256]{2,0,1:T(8,128)S(1)} copy(f32[16,128,256]{1,2,0:T(8,128)} %convolution_bitcast_fusion) | data formatting | bytes 4194304 | tf_op jit(solution)/shard_map/sij,sjd->sid/dot_general | solution.py:61
  107.9 2.5 %fusion.51 = f32[16,128,256]{2,0,1:T(8,128)S(1)} fusion(f32[16,128,256]{2,0,1:T(8,128)S(1)} %copy.246, f32[16]{0:T(128)} %copy-done.10, s32[16]{0:T(128)S(1)} %eq.45), kind=kOutput, calls=%fused_computation.190 | convolution fusion | flops 100663808 | bytes 4194432 | tf_op jit(solution)/shard_map/sn,sid->nid/dot_general | solution.py:64
  110.4 1.2 copy.247
  111.6 1.9 copy.248
  113.5 6.0 %multiply_convert_fusion.1 = (bf16[2048,256]{1,0:T(8,128)(2,1)S(1)}, bf16[2048,256]{1,0:T(8,128)(2,1)}) fusion(bf16[2048,256]{1,0:T(8,128)(2,1)} %param.21, f32[256]{0:T(256)S(1)} %copy-done.13, f32[2048,256]{1,0:T(8,128)} %fusion.70, bf16[256,256]{1,0:T(8,128)(2,1)S(1)} %copy-done, f32[2048,256]{0,1:T(8,128)} %copy.248, ...), kind=kOutput, calls=%fused_computation.18 | convolution fusion | flops 546308096 | bytes 10757120 | tf_op jit(solution)/shard_map/dot_general | solution.py:75
  120.4 2.1 fusion.9
  122.6 1.7 fusion.11
  124.3 1.7 fusion.13
  126.1 1.7 fusion.15
  127.8 1.7 fusion.17
  129.6 1.7 fusion.19
  150.9 5.1 %all-to-all-start.3 = ((bf16[32,6,1,8,256]{4,3,1,2,0:T(8,128)(2,1)}), bf16[32,6,1,8,256]{4,3,1,2,0:T(8,128)(2,1)S(1)}, u32[]{:S(2)}, u32[]{:S(2)}) async-start(bf16[32,6,1,8,256]{4,3,1,2,0:T(8,128)(2,1)} %constant_dynamic-update-slice_fusion.38), calls=%async_computation.3 | async-start | bytes 1572864 | tf_op jit(solution)/shard_map/all_to_all | solution.py:95
  156.6 1.4 multiply_convert_fusion
  158.0 12.2 %all-to-all-done.3 = bf16[32,6,1,8,256]{4,3,1,2,0:T(8,128)(2,1)S(1)} async-done(((bf16[32,6,1,8,256]{4,3,1,2,0:T(8,128)(2,1)}), bf16[32,6,1,8,256]{4,3,1,2,0:T(8,128)(2,1)S(1)}, u32[]{:S(2)}, u32[]{:S(2)}) %all-to-all-start.3) | async-done | bytes 786464 | tf_op jit(solution)/shard_map/all_to_all | solution.py:95
  170.2 6.9 %all-to-all-start.2 = ((bf16[8,2,128,256]{2,3,1,0:T(8,128)(2,1)}), bf16[8,2,128,256]{2,3,1,0:T(8,128)(2,1)S(1)}, u32[]{:S(2)}, u32[]{:S(2)}) async-start(bf16[8,2,128,256]{2,3,1,0:T(8,128)(2,1)} %bitcast.98), calls=%async_computation.2 | async-start | bytes 2097152 | tf_op jit(solution)/shard_map/all_to_all | solution.py:112
  178.2 28.2 %all-to-all-done.2 = bf16[8,2,128,256]{2,3,1,0:T(8,128)(2,1)S(1)} async-done(((bf16[8,2,128,256]{2,3,1,0:T(8,128)(2,1)}), bf16[8,2,128,256]{2,3,1,0:T(8,128)(2,1)S(1)}, u32[]{:S(2)}, u32[]{:S(2)}) %all-to-all-start.2) | async-done | bytes 1048608 | tf_op jit(solution)/shard_map/all_to_all | solution.py:112
  206.4 4.3 %all-to-all-start.4 = ((bf16[32,8,256]{2,1,0:T(8,128)(2,1)}), bf16[32,8,256]{2,1,0:T(8,128)(2,1)S(1)}, u32[]{:S(2)}, u32[]{:S(2)}) async-start(bf16[32,8,256]{2,1,0:T(8,128)(2,1)} %multiply_reduce_fusion), calls=%async_computation.4 | async-start | bytes 262144 | tf_op jit(solution)/shard_map/all_to_all | solution.py:101
  212.1 1.2 copy.283
  213.3 5.0 %all-to-all-done.4 = bf16[32,8,256]{2,1,0:T(8,128)(2,1)S(1)} async-done(((bf16[32,8,256]{2,1,0:T(8,128)(2,1)}), bf16[32,8,256]{2,1,0:T(8,128)(2,1)S(1)}, u32[]{:S(2)}, u32[]{:S(2)}) %all-to-all-start.4) | async-done | bytes 131104 | tf_op jit(solution)/shard_map/all_to_all | solution.py:101
  218.3 1.4 fusion.4
  (123 shorter events, 35.9 us)
Async XLA Ops:
  0.6 112.9 %copy-start = (bf16[256,256]{1,0:T(8,128)(2,1)S(1)}, bf16[256,256]{1,0:T(8,128)(2,1)}, u32[]{:S(2)}) copy-start(bf16[256,256]{1,0:T(8,128)(2,1)} %param.13) | copy-start | bytes 393220
  0.6 50.1 %copy-start.1 = (bf16[2048,256]{1,0:T(8,128)(2,1)S(1)}, bf16[2048,256]{1,0:T(8,128)(2,1)}, u32[]{:S(2)}) copy-start(bf16[2048,256]{1,0:T(8,128)(2,1)} %param.11) | copy-start | bytes 3145732
  2.3 59.8 %all-to-all-start.1 = ((bf16[32,8,256]{2,1,0:T(8,128)(2,1)}), bf16[32,8,256]{2,1,0:T(8,128)(2,1)S(1)}, u32[]{:S(2)}, u32[]{:S(2)}) async-start(bf16[32,8,256]{2,1,0:T(8,128)(2,1)} %slice_bitcast_fusion.13), calls=%async_computation.1 | async-start | bytes 262144 | tf_op jit(solution)/shard_map/all_to_all | solution.py:31
  43.1 9.2 %copy-start.12 = (s32[1,8]{1,0:T(1,128)S(1)}, s32[1,8]{1,0:T(1,128)}, u32[]{:S(2)}) copy-start(s32[1,8]{1,0:T(1,128)} %param.18) | copy-start | bytes 100
  43.1 9.3 %copy-start.2 = (bf16[1,8,2,128,128]{4,3,2,1,0:T(8,128)(2,1)S(1)}, bf16[1,8,2,128,128]{4,3,2,1,0:T(8,128)(2,1)}, u32[]{:S(2)}) copy-start(bf16[1,8,2,128,128]{4,3,2,1,0:T(8,128)(2,1)} %param.20) | copy-start | bytes 1572868
  52.4 9.6 %copy-start.10 = (f32[16]{0:T(128)}, f32[16]{0:T(128)S(1)}, u32[]{:S(2)}) copy-start(f32[16]{0:T(128)S(1)} %reshape.211) | copy-start | bytes 196
  52.6 3.7 %copy-start.7 = (bf16[256,256]{1,0:T(8,128)(2,1)S(1)}, bf16[256,256]{1,0:T(8,128)(2,1)}, u32[]{:S(2)}) copy-start(bf16[256,256]{1,0:T(8,128)(2,1)} %param.12) | copy-start | bytes 393220
  62.2 37.6 %slice-start = ((s8[6291456]{0:T(1024)(128)(4,1)}), s8[2097152]{0:T(1024)(128)(4,1)S(1)}, s32[]{:S(2)}) async-start(s8[6291456]{0:T(1024)(128)(4,1)} %bitcast.443), calls=%async_computation.5 | async-start | bytes 4194304
  62.2 40.4 %all-to-all-start = ((bf16[8,2,128,256]{2,3,1,0:T(8,128)(2,1)}), bf16[8,2,128,256]{2,3,1,0:T(8,128)(2,1)}, u32[]{:S(2)}, u32[]{:S(2)}) async-start(bf16[8,2,128,256]{2,3,1,0:T(8,128)(2,1)} %copy.245), calls=%async_computation | async-start | bytes 2097152 | tf_op jit(solution)/shard_map/all_to_all | solution.py:50
  96.1 3.6 %slice-start.1 = ((s8[6291456]{0:T(1024)(128)(4,1)}), s8[4194304]{0:T(1024)(128)(4,1)S(1)}, s32[]{:S(2)}) async-start(s8[6291456]{0:T(1024)(128)(4,1)} %bitcast.443), calls=%async_computation.6 | async-start | bytes 8388608
  111.6 1.9 copy-start.13
  119.5 1.0 copy-start.3
  120.4 9.2 %copy-start.5 = (bf16[2048,256]{0,1:T(8,128)(2,1)}, bf16[2048,256]{0,1:T(8,128)(2,1)S(1)}, u32[]{:S(2)}) copy-start(bf16[2048,256]{0,1:T(8,128)(2,1)S(1)} %fusion.5) | copy-start | bytes 3145732
  131.4 24.6 %copy-start.6 = (bf16[2048,256]{0,1:T(8,128)(2,1)S(1)}, bf16[2048,256]{0,1:T(8,128)(2,1)}, u32[]{:S(2)}) copy-start(bf16[2048,256]{0,1:T(8,128)(2,1)} %copy-done.5) | copy-start | bytes 3145732
  144.8 11.9 %copy-start.11 = (f32[16]{0:T(128)S(1)}, f32[16]{0:T(128)}, u32[]{:S(2)}) copy-start(f32[16]{0:T(128)} %copy-done.10) | copy-start | bytes 196
  150.9 19.3 %all-to-all-start.3 = ((bf16[32,6,1,8,256]{4,3,1,2,0:T(8,128)(2,1)}), bf16[32,6,1,8,256]{4,3,1,2,0:T(8,128)(2,1)S(1)}, u32[]{:S(2)}, u32[]{:S(2)}) async-start(bf16[32,6,1,8,256]{4,3,1,2,0:T(8,128)(2,1)} %constant_dynamic-update-slice_fusion.38), calls=%async_computation.3 | async-start | bytes 1572864 | tf_op jit(solution)/shard_map/all_to_all | solution.py:95
  156.6 20.5 %copy-start.9 = (s32[6]{0:T(128)S(1)}, s32[6]{0:T(128)}, u32[]{:S(2)}) copy-start(s32[6]{0:T(128)} %param.15) | copy-start | bytes 76
  170.2 36.2 %all-to-all-start.2 = ((bf16[8,2,128,256]{2,3,1,0:T(8,128)(2,1)}), bf16[8,2,128,256]{2,3,1,0:T(8,128)(2,1)S(1)}, u32[]{:S(2)}, u32[]{:S(2)}) async-start(bf16[8,2,128,256]{2,3,1,0:T(8,128)(2,1)} %bitcast.98), calls=%async_computation.2 | async-start | bytes 2097152 | tf_op jit(solution)/shard_map/all_to_all | solution.py:112
  206.4 12.0 %all-to-all-start.4 = ((bf16[32,8,256]{2,1,0:T(8,128)(2,1)}), bf16[32,8,256]{2,1,0:T(8,128)(2,1)S(1)}, u32[]{:S(2)}, u32[]{:S(2)}) async-start(bf16[32,8,256]{2,1,0:T(8,128)(2,1)} %multiply_reduce_fusion), calls=%async_computation.4 | async-start | bytes 262144 | tf_op jit(solution)/shard_map/all_to_all | solution.py:101
  212.0 6.3 %copy-start.4 = (bf16[2048,256]{1,0:T(8,128)(2,1)S(1)}, bf16[2048,256]{1,0:T(8,128)(2,1)}, u32[]{:S(2)}) copy-start(bf16[2048,256]{1,0:T(8,128)(2,1)} %copy-done.3) | copy-start | bytes 3145732
  212.0 6.3 %copy-start.8 = (bf16[256,256]{1,0:T(8,128)(2,1)S(1)}, bf16[256,256]{1,0:T(8,128)(2,1)}, u32[]{:S(2)}) copy-start(bf16[256,256]{1,0:T(8,128)(2,1)} %param.12) | copy-start | bytes 393220
